TPU v7x, 512 devices: a whole 4x4x16 slice. The times are simulated.
512 devices in a mesh: wide: 64 (over y_hi, z, core), narrow: 8 (over x, y_lo).
Axes of the slice: x: 4, y: 4 (y_hi: 2, y_lo: 2; y = y_hi * 2 + y_lo), z: 16, core: 2. Of those that a mesh axis runs over, the one named last changes fastest.
Arguments:
- examples: bfloat16 [320, 8192], P('wide', 'narrow'), may hold values from -6 to 6
- references: bfloat16 [128, 8192], P('wide', 'narrow'), may hold values from -6 to 6
- gate_weight: bfloat16 [8192, 28672], P('narrow', 'wide'), may hold values from -0.0625 to 0.0625
- up_weight: bfloat16 [8192, 28672], P('narrow', 'wide'), may hold values from -0.0625 to 0.0625
- down_weight: bfloat16 [28672, 8192], P('wide', 'narrow'), may hold values from -0.03125 to 0.03125
- cotangent: bfloat16 [320, 8192], P('wide', 'narrow'), may hold values from -6 to 6
- pair_ref: int32 [320, 4], replicated, may hold values from 0 to 127
- points: int32 [8], replicated, may hold values from 1 to 8
Outputs:
- expected: bfloat16 [320, 8192], P('wide', 'narrow')
All inputs are finite; a program needn't handle non-finite values.
Results may differ from a plain program's by a relative error of at most 0.005.
Values may be sent and summed in bfloat16 or wider, within the bound.
A program may use at most 64 MiB of HBM per device.

v0:
```python
import jax
import jax.numpy as jnp
from jax import lax
from jax.sharding import Mesh
from jax.sharding import PartitionSpec as P

WIDE = ("wide_0", "wide_1", "wide_2")


def copy_for_each(x, axis):
    size = lax.axis_size(axis)
    return lax.all_to_all(jnp.broadcast_to(x[None], (size, *x.shape)), axis, 0, 0, tiled=True)


def in_order(blocks, dim):
    blocks = jnp.moveaxis(blocks, 0, dim)
    dims = blocks.shape
    return blocks.reshape(*dims[:dim], dims[dim] * dims[dim + 1], *dims[dim + 2 :])


def gather_axes(x, axes, dim):
    far, near = axes
    blocks = copy_for_each(copy_for_each(x, far), near)
    return in_order(blocks.swapaxes(0, 1).reshape(-1, *x.shape), dim)


def cut_along(x, dim, size):
    before, after = (x.shape[:dim], x.shape[dim + 1 :])
    return jnp.moveaxis(x.reshape(*before, size, -1, *after), dim, 0)


def summed_on_arrival(x, axis, dim):
    blocks = cut_along(x, dim, lax.axis_size(axis))
    arrived = lax.all_to_all(blocks, axis, split_axis=0, concat_axis=0, tiled=True)
    return arrived.sum(axis=0)


def sent_together(arrays, axis, dim, along):
    both = jnp.concatenate(arrays, axis=along)
    out, at, outs = (summed_on_arrival(both, axis, dim), 0, [])
    for a in arrays:
        outs.append(lax.slice_in_dim(out, at, at + a.shape[along], axis=along))
        at += a.shape[along]
    return tuple(outs)


def turned_gather(arrays, axis, dims):
    turned = [jnp.moveaxis(a, dim, 0) for a, dim in zip(arrays, dims)]
    widths = [t[0].size for t in turned]
    both = jnp.concatenate([t.reshape(-1, w) for t, w in zip(turned, widths)], axis=1)
    out = lax.all_gather(both, axis, axis=0, tiled=True)
    blocks = jnp.split(out, [sum(widths[:k]) for k in range(1, len(widths))], axis=1)
    return tuple(
        (
            jnp.moveaxis(b.reshape(-1, *t.shape[1:]), 0, dim)
            for b, t, dim in zip(blocks, turned, dims)
        )
    )


def sum_in_two_steps(x, axes, dim):
    far, near = axes
    own = summed_on_arrival(cut_along(x, dim, lax.axis_size(far)), near, dim + 1)
    return jnp.sum(lax.all_to_all(own, far, 0, 0, tiled=True), axis=0)


def path_coefficients(example_gate, example_up, reference_gate, reference_up, pair_ref, points):
    alphas = points.astype(jnp.float32) / 8.0
    coef_gate = jnp.zeros(example_gate.shape, jnp.float32)
    coef_up = jnp.zeros(example_gate.shape, jnp.float32)
    for pair_slot in range(pair_ref.shape[1]):
        chosen = pair_ref[:, pair_slot]
        base_gate = jnp.take(reference_gate, chosen, axis=0)
        base_up = jnp.take(reference_up, chosen, axis=0)
        step_gate = example_gate - base_gate
        step_up = example_up - base_up
        for point_slot in range(alphas.shape[0]):
            position = alphas[point_slot]
            along_gate = base_gate + position * step_gate
            along_up = base_up + position * step_up
            sigmoid = jax.nn.sigmoid(along_gate)
            coef_gate = coef_gate + along_up * sigmoid * (1.0 + along_gate * (1.0 - sigmoid))
            coef_up = coef_up + along_gate * sigmoid
    total = pair_ref.shape[1] * alphas.shape[0]
    return (coef_gate / total, coef_up / total)


def transposed_product(left, right):
    return lax.dot_general(
        left, right, (((1,), (1,)), ((), ())), preferred_element_type=jnp.float32
    )


def on_device(
    examples, references, gate_weight, up_weight, down_weight, cotangent, pair_ref, points
):
    all_examples, all_references, all_cotangent = (
        gather_axes(examples, (("wide_0", "wide_1"), "wide_2"), 0),
        gather_axes(references, (("wide_0", "wide_1"), "wide_2"), 0),
        gather_axes(cotangent, (("wide_0", "wide_1"), "wide_2"), 0),
    )
    gate_terms = jnp.dot(all_examples, gate_weight, preferred_element_type=jnp.float32)
    up_terms = jnp.dot(all_examples, up_weight, preferred_element_type=jnp.float32)
    reference_gate_terms = jnp.dot(all_references, gate_weight, preferred_element_type=jnp.float32)
    reference_up_terms = jnp.dot(all_references, up_weight, preferred_element_type=jnp.float32)
    upstream_terms = transposed_product(all_cotangent, down_weight)
    example_gate, example_up, reference_gate, reference_up, upstream = sent_together(
        (gate_terms, up_terms, reference_gate_terms, reference_up_terms, upstream_terms),
        "narrow",
        1,
        0,
    )
    coef_gate, coef_up = path_coefficients(
        example_gate, example_up, reference_gate, reference_up, pair_ref, points
    )
    grad_gate = (upstream * coef_gate).astype(jnp.bfloat16)
    grad_up = (upstream * coef_up).astype(jnp.bfloat16)
    full_gate, full_up = turned_gather((grad_gate, grad_up), "narrow", (1, 1))
    result = sum_in_two_steps(
        transposed_product(full_gate, gate_weight) + transposed_product(full_up, up_weight),
        (("wide_0", "wide_1"), "wide_2"),
        0,
    )
    return result.astype(jnp.bfloat16)


def solution(mesh):
    split = Mesh(
        mesh.devices.reshape(2, 16, 2, mesh.shape["narrow"]),
        ("wide_0", "wide_1", "wide_2", "narrow"),
    )
    placed = (
        P(WIDE, "narrow"),
        P(WIDE, "narrow"),
        P("narrow", WIDE),
        P("narrow", WIDE),
        P(WIDE, "narrow"),
        P(WIDE, "narrow"),
        P(),
        P(),
    )
    return jax.shard_map(
        on_device, mesh=split, in_specs=placed, out_specs=P(WIDE, "narrow"), check_vma=False
    )
```

profile of v0, /device:TPU:32, one launch (start us, length us, event | category | flops | bytes accessed | tf_op | source)
XLA Modules:
  0.0 296.1 jit_solution(9119121526575013563)
XLA Ops:
  0.0 0.8 broadcast_in_dim.20
  0.8 35.1 %all_to_all.45 = bf16[32,2,1024]{2,1,0:T(2,128)(2,1)S(1)} all-to-all(bf16[32,2,1024]{2,1,0:T(2,128)(2,1)S(1)} %broadcast_in_dim.20), channel_id=1, replica_groups=mesh['wide_0'=2,'wide_1'=16,'wide_2'=2,'narrow'=8] {'wide_0','wide_1'}, dimensions={0} | all-to-all | bytes 262144 | tf_op jit(solution)/shard_map/all_to_all | solution.py:12
  36.0 0.8 broadcast_in_dim.18
  36.8 37.0 %all_to_all.46 = bf16[32,5,1024]{2,1,0:T(8,128)(2,1)S(1)} all-to-all(bf16[32,5,1024]{2,1,0:T(8,128)(2,1)S(1)} %broadcast_in_dim.18), channel_id=1, replica_groups=mesh['wide_0'=2,'wide_1'=16,'wide_2'=2,'narrow'=8] {'wide_0','wide_1'}, dimensions={0} | all-to-all | bytes 655360 | tf_op jit(solution)/shard_map/all_to_all | solution.py:12
  73.7 0.8 broadcast_in_dim.21
  74.6 3.4 %all-to-all-start.3 = ((bf16[2,32,2,1024]{3,2,1,0:T(2,128)(2,1)}), bf16[2,32,2,1024]{3,2,1,0:T(2,128)(2,1)S(1)}, u32[]{:S(2)}, u32[]{:S(2)}) async-start(bf16[2,32,2,1024]{3,2,1,0:T(2,128)(2,1)} %broadcast_in_dim.21), calls=%async_computation.3 | async-start | bytes 524288 | tf_op jit(solution)/shard_map/all_to_all | solution.py:12
  78.0 0.2 copy.61
  78.2 1.3 all-to-all-done.3
  79.5 0.1 broadcast_in_dim.19
  79.6 4.3 %all_to_all.47 = bf16[2,32,5,1024]{3,1,2,0:T(8,128)(2,1)S(1)} all-to-all(bf16[2,32,5,1024]{3,1,2,0:T(8,128)(2,1)S(1)} %broadcast_in_dim.19), channel_id=1, replica_groups=mesh['wide_0'=2,'wide_1'=16,'wide_2'=2,'narrow'=8] {'wide_2'}, dimensions={0} | all-to-all | bytes 1310720 | tf_op jit(solution)/shard_map/all_to_all | solution.py:12
  83.9 0.9 broadcast_in_dim.22
  84.7 4.4 %all-to-all-start.4 = ((bf16[32,5,1024]{2,1,0:T(8,128)(2,1)}), bf16[32,5,1024]{2,1,0:T(8,128)(2,1)}, u32[]{:S(2)}, u32[]{:S(2)}) async-start(bf16[32,5,1024]{2,1,0:T(8,128)(2,1)} %broadcast_in_dim.22), calls=%async_computation.4 | async-start | bytes 1048576 | tf_op jit(solution)/shard_map/all_to_all | solution.py:12
  89.2 0.2 copy.63
  89.3 0.8 reshape_reshape.13
  90.2 0.4 copy.62
  90.5 0.3 reshape_reshape.12
  90.8 1.4 convolution_dynamic-update-slice_fusion.2
  92.2 1.4 convolution_dynamic-update-slice_fusion.1
  93.6 1.2 convolution_dynamic-update-slice_fusion.4
  94.8 1.1 convolution_dynamic-update-slice_fusion.3
  95.9 27.4 %all-to-all-done.4 = bf16[32,5,1024]{2,1,0:T(8,128)(2,1)} async-done(((bf16[32,5,1024]{2,1,0:T(8,128)(2,1)}), bf16[32,5,1024]{2,1,0:T(8,128)(2,1)}, u32[]{:S(2)}, u32[]{:S(2)}) %all-to-all-start.4) | async-done | bytes 327712 | tf_op jit(solution)/shard_map/all_to_all | solution.py:12
  123.3 1.3 copy.64
  124.6 0.1 broadcast_in_dim.23
  124.7 4.4 %all_to_all.48 = bf16[2,32,5,1024]{3,1,2,0:T(8,128)(2,1)S(1)} all-to-all(bf16[2,32,5,1024]{3,1,2,0:T(8,128)(2,1)S(1)} %broadcast_in_dim.23), channel_id=1, replica_groups=mesh['wide_0'=2,'wide_1'=16,'wide_2'=2,'narrow'=8] {'wide_2'}, dimensions={0} | all-to-all | bytes 1310720 | tf_op jit(solution)/shard_map/all_to_all | solution.py:12
  129.1 0.4 copy.65
  129.4 0.3 reshape_reshape.14
  129.7 1.4 convolution_dynamic-update-slice_fusion
  131.1 3.1 %copy.68 = f32[1216,448]{0,1:T(8,128)} copy(f32[1216,448]{1,0:T(8,128)} %convolution_dynamic-update-slice_fusion) | data formatting | bytes 4358144 | tf_op jit(solution)/shard_map/concatenate | solution.py:39
  134.2 4.5 %all-to-all-start.6 = ((f32[8,1216,56]{1,2,0:T(8,128)}), f32[8,1216,56]{1,2,0:T(8,128)S(1)}, u32[]{:S(2)}, u32[]{:S(2)}) async-start(f32[8,1216,56]{1,2,0:T(8,128)} %bitcast.31), calls=%async_computation.6 | async-start | bytes 4587520 | tf_op jit(solution)/shard_map/all_to_all | solution.py:34
  138.9 0.7 fusion.17
  139.6 33.5 %all-to-all-done.6 = f32[8,1216,56]{1,2,0:T(8,128)S(1)} async-done(((f32[8,1216,56]{1,2,0:T(8,128)}), f32[8,1216,56]{1,2,0:T(8,128)S(1)}, u32[]{:S(2)}, u32[]{:S(2)}) %all-to-all-start.6) | async-done | bytes 2179104 | tf_op jit(solution)/shard_map/all_to_all | solution.py:34
  173.1 0.1 reduce_sum.27
  173.3 0.1 copy.84
  173.4 1.1 gather_fusion.3
  174.5 1.1 gather_fusion.1
  175.6 0.1 copy.83
  175.6 1.1 gather_fusion
  176.7 1.1 gather_fusion.2
  177.8 1.1 gather_fusion.5
  178.9 1.1 gather_fusion.4
  180.0 1.1 gather_fusion.7
  181.1 1.1 gather_fusion.6
  182.2 0.1 copy.74
  182.3 0.1 copy.76
  182.4 0.1 copy.78
  182.5 0.1 copy.72
  182.6 0.1 copy.70
  182.8 0.1 copy.73
  182.9 0.1 copy.75
  183.0 0.1 copy.77
  183.1 5.7 %fusion.14 = bf16[56,320]{1,0:T(8,128)(2,1)S(1)} fusion(f32[1216,56]{0,1:T(8,128)S(1)} %reduce_sum.27, f32[]{:T(128)} %bitcast.5, f32[320,56]{0,1:T(8,128)S(1)} %copy.72, pred[320]{0:T(512)(128)(4,1)S(1)} %get-tuple-element.27, f32[]{:T(128)} %bitcast.6, f32[]{:T(128)} %bitcast.7, f32[]{:T(128)} %bitcast.8, f32[]{:T(128)} %bitcast.9, f32[]{:T(128)} %bitcast.10, ...), kind=kLoop, calls=%fused_computation.102 | loop fusion | flops 4193280 | bytes 467232 | tf_op jit(solution)/shard_map/transpose | solution.py:48
  188.8 0.0 copy-start.2
  188.8 6.3 %fusion.15 = bf16[56,320]{1,0:T(8,128)(2,1)S(1)} fusion(f32[320,56]{0,1:T(8,128)S(1)} %copy.77, pred[320]{0:T(512)(128)(4,1)S(1)} %get-tuple-element.24, f32[320,56]{0,1:T(8,128)S(1)} %copy.75, pred[320]{0:T(512)(128)(4,1)S(1)} %get-tuple-element.25, f32[320,56]{0,1:T(8,128)S(1)} %copy.73, pred[320]{0:T(512)(128)(4,1)S(1)} %get-tuple-element.26, ...), kind=kLoop, calls=%fused_computation.103 | loop fusion | flops 7777280 | bytes 825632 | tf_op jit(solution)/shard_map/transpose | solution.py:48
  195.2 0.1 pad_maximum_fusion
  195.3 29.4 %all_gather.3 = bf16[448,640]{1,0:T(8,128)(2,1)S(1)} all-gather(bf16[56,640]{1,0:T(8,128)(2,1)S(1)} %pad_maximum_fusion), channel_id=1, replica_groups=mesh['wide_0'=2,'wide_1'=16,'wide_2'=2,'narrow'=8] {'narrow'}, dimensions={0}, use_global_device_ids=true | all-gather | bytes 645120 | tf_op jit(solution)/shard_map/all_gather | solution.py:51
  224.6 0.5 fusion.1
  225.2 1.8 convolution_add_fusion
  226.9 1.4 reshape_reshape.15
  228.3 0.8 copy.79
  229.1 4.8 %all_to_all.49 = f32[2,32,5,1024]{3,1,2,0:T(8,128)S(1)} all-to-all(f32[2,32,5,1024]{3,1,2,0:T(8,128)S(1)} %copy.79), channel_id=1, replica_groups=mesh['wide_0'=2,'wide_1'=16,'wide_2'=2,'narrow'=8] {'wide_2'}, dimensions={0} | all-to-all | bytes 2621440 | tf_op jit(solution)/shard_map/all_to_all | solution.py:34
  233.9 0.1 reduce_sum.28
  234.0 0.4 copy.80
  234.4 61.0 %all_to_all.50 = f32[32,5,1024]{2,1,0:T(8,128)S(1)} all-to-all(f32[32,5,1024]{2,1,0:T(8,128)S(1)} %copy.80), channel_id=1, replica_groups=mesh['wide_0'=2,'wide_1'=16,'wide_2'=2,'narrow'=8] {'wide_0','wide_1'}, dimensions={0} | all-to-all | bytes 1310720 | tf_op jit(solution)/shard_map/all_to_all | solution.py:64
  295.5 0.7 reduce_sum.29
  (26 shorter events, 0.1 us)
Async XLA Ops:
  0.0 90.8 %copy-start = (bf16[1024,448]{0,1:T(8,128)(2,1)S(1)}, bf16[1024,448]{0,1:T(8,128)(2,1)}, u32[]{:S(2)}) copy-start(bf16[1024,448]{0,1:T(8,128)(2,1)} %param.12) | copy-start | bytes 2752516
  36.8 47.1 %copy-start.5 = (bf16[5,1024]{1,0:T(8,128)(2,1)S(1)}, bf16[5,1024]{1,0:T(8,128)(2,1)}, u32[]{:S(2)}) copy-start(bf16[5,1024]{1,0:T(8,128)(2,1)} %param.15) | copy-start | bytes 30724
  74.6 5.0 %all-to-all-start.3 = ((bf16[2,32,2,1024]{3,2,1,0:T(2,128)(2,1)}), bf16[2,32,2,1024]{3,2,1,0:T(2,128)(2,1)S(1)}, u32[]{:S(2)}, u32[]{:S(2)}) async-start(bf16[2,32,2,1024]{3,2,1,0:T(2,128)(2,1)} %broadcast_in_dim.21), calls=%async_computation.3 | async-start | bytes 524288 | tf_op jit(solution)/shard_map/all_to_all | solution.py:12
  84.7 38.6 %all-to-all-start.4 = ((bf16[32,5,1024]{2,1,0:T(8,128)(2,1)}), bf16[32,5,1024]{2,1,0:T(8,128)(2,1)}, u32[]{:S(2)}, u32[]{:S(2)}) async-start(bf16[32,5,1024]{2,1,0:T(8,128)(2,1)} %broadcast_in_dim.22), calls=%async_computation.4 | async-start | bytes 1048576 | tf_op jit(solution)/shard_map/all_to_all | solution.py:12
  90.2 2.1 copy-start.1
  90.8 2.8 copy-start.3
  124.6 5.1 %copy-start.4 = (bf16[448,1024]{1,0:T(8,128)(2,1)S(1)}, bf16[448,1024]{1,0:T(8,128)(2,1)}, u32[]{:S(2)}) copy-start(bf16[448,1024]{1,0:T(8,128)(2,1)} %param.14) | copy-start | bytes 2752516
  134.2 4.6 %copy-start.6 = (s32[320,4]{0,1:T(4,128)S(1)}, s32[320,4]{0,1:T(4,128)}, u32[]{:S(2)}) copy-start(s32[320,4]{0,1:T(4,128)} %param.16) | copy-start | bytes 15364
  134.2 4.7 %copy-start.7 = (s32[8]{0:T(128)S(1)}, s32[8]{0:T(128)}, u32[]{:S(2)}) copy-start(s32[8]{0:T(128)} %param.17) | copy-start | bytes 100
  134.2 38.9 %all-to-all-start.6 = ((f32[8,1216,56]{1,2,0:T(8,128)}), f32[8,1216,56]{1,2,0:T(8,128)S(1)}, u32[]{:S(2)}, u32[]{:S(2)}) async-start(f32[8,1216,56]{1,2,0:T(8,128)} %bitcast.31), calls=%async_computation.6 | async-start | bytes 4587520 | tf_op jit(solution)/shard_map/all_to_all | solution.py:34
  188.8 36.3 %copy-start.2 = (bf16[1024,448]{0,1:T(8,128)(2,1)S(1)}, bf16[1024,448]{0,1:T(8,128)(2,1)}, u32[]{:S(2)}) copy-start(bf16[1024,448]{0,1:T(8,128)(2,1)} %param.13) | copy-start | bytes 2752516
where the time goes:
time: 297 us; the launch traced here: 296 us
  blocking collectives  176 us (59%)
  waiting for transfers between devices  62.2 us (21%)
  local copies, waits for them, and re-layouts  23.4 us (8%)
  other arithmetic  13.2 us (4%)
  starting transfers between devices  12.4 us (4%)
  matrix products  8.71 us (3%)
    all_to_all x4, blocking collectives, copy_for_each(): lax.all_to_all(jnp.broadcast_to(x[None], (size, *x.shape)), axis, 0, 0, t...  80.7 us
    all_to_all x1, blocking collectives, sum_in_two_steps(): return jnp.sum(lax.all_to_all(own, far, 0, 0, tiled=True), axis=0)  61 us
    all_to_all x1, waiting for transfers between devices, summed_on_arrival(): lax.all_to_all(blocks, axis, split_axis=0, concat_axis=0, tiled=True)  33.5 us
    all_gather x1, blocking collectives, turned_gather(): out = lax.all_gather(both, axis, axis=0, tiled=True)  29.4 us
    all_to_all x2, waiting for transfers between devices, copy_for_each(): lax.all_to_all(jnp.broadcast_to(x[None], (size, *x.shape)), axis, 0, 0, t...  28.7 us
    transpose x2, other arithmetic, turned_gather(): turned = [jnp.moveaxis(a, dim, 0) for a, dim in zip(arrays, dims)]  12.1 us
    all_to_all x2, starting transfers between devices, copy_for_each(): lax.all_to_all(jnp.broadcast_to(x[None], (size, *x.shape)), axis, 0, 0, t...  7.84 us
  transfers between devices with their start and end apart: 3, of which 3 were waited for; matrix products, arithmetic and copies ran while one was open for 3% of the time, Pallas kernels for 0%

commit v1 on v0

--- a/solution.py
+++ b/solution.py
@@ -48,7 +48,10 @@
     turned = [jnp.moveaxis(a, dim, 0) for a, dim in zip(arrays, dims)]
     widths = [t[0].size for t in turned]
     both = jnp.concatenate([t.reshape(-1, w) for t, w in zip(turned, widths)], axis=1)
-    out = lax.all_gather(both, axis, axis=0, tiled=True)
+    count = lax.axis_size(axis)
+    shards = jnp.stack([both for _ in range(count)])
+    shards = lax.all_to_all(shards, axis, split_axis=0, concat_axis=0)
+    out = jnp.concatenate(shards, axis=0)
     blocks = jnp.split(out, [sum(widths[:k]) for k in range(1, len(widths))], axis=1)
     return tuple(
         (

time: 297 us -> 280 us (0.943)
  blocking collectives: 176 us -> 159 us
    all_gather x1 -> x0, blocking collectives: 29.4 us -> none  [turned_gather(): out = lax.all_gather(both, axis, axis=0, tiled=True)]
    all_to_all x0 -> x1, blocking collectives: none -> 12.9 us  [turned_gather(): shards = lax.all_to_all(shards, axis, split_axis=0, concat_axis=0)]
where the time goes in v1:
time: 280 us
  blocking collectives  159 us (57%)
  waiting for transfers between devices  62.2 us (22%)
  local copies, waits for them, and re-layouts  23.4 us (8%)
  other arithmetic  13.1 us (5%)
  starting transfers between devices  12.4 us (4%)
  matrix products  8.71 us (3%)
    all_to_all x4, blocking collectives, copy_for_each(): lax.all_to_all(jnp.broadcast_to(x[None], (size, *x.shape)), axis, 0, 0, t...  80.7 us
    all_to_all x1, blocking collectives, sum_in_two_steps(): return jnp.sum(lax.all_to_all(own, far, 0, 0, tiled=True), axis=0)  60.9 us
    all_to_all x1, waiting for transfers between devices, summed_on_arrival(): lax.all_to_all(blocks, axis, split_axis=0, concat_axis=0, tiled=True)  33.5 us
    all_to_all x2, waiting for transfers between devices, copy_for_each(): lax.all_to_all(jnp.broadcast_to(x[None], (size, *x.shape)), axis, 0, 0, t...  28.7 us
    all_to_all x1, blocking collectives, turned_gather(): shards = lax.all_to_all(shards, axis, split_axis=0, concat_axis=0)  12.9 us
    transpose x2, other arithmetic, turned_gather(): turned = [jnp.moveaxis(a, dim, 0) for a, dim in zip(arrays, dims)]  12 us
    all_to_all x2, starting transfers between devices, copy_for_each(): lax.all_to_all(jnp.broadcast_to(x[None], (size, *x.shape)), axis, 0, 0, t...  7.84 us
  transfers between devices with their start and end apart: 3, of which 3 were waited for; matrix products, arithmetic and copies ran while one was open for 3% of the time, Pallas kernels for 0%

profile of v1, /device:TPU:32, one launch (start us, length us, event | category | flops | bytes accessed | tf_op | source)
XLA Modules:
  0.0 279.5 jit_solution(11706142127028885322)
XLA Ops:
  0.0 0.8 broadcast_in_dim.20
  0.8 35.1 %all_to_all.50 = bf16[32,2,1024]{2,1,0:T(2,128)(2,1)S(1)} all-to-all(bf16[32,2,1024]{2,1,0:T(2,128)(2,1)S(1)} %broadcast_in_dim.20), channel_id=1, replica_groups=mesh['wide_0'=2,'wide_1'=16,'wide_2'=2,'narrow'=8] {'wide_0','wide_1'}, dimensions={0} | all-to-all | bytes 262144 | tf_op jit(solution)/shard_map/all_to_all | solution.py:12
  36.0 0.8 broadcast_in_dim.18
  36.8 37.0 %all_to_all.51 = bf16[32,5,1024]{2,1,0:T(8,128)(2,1)S(1)} all-to-all(bf16[32,5,1024]{2,1,0:T(8,128)(2,1)S(1)} %broadcast_in_dim.18), channel_id=1, replica_groups=mesh['wide_0'=2,'wide_1'=16,'wide_2'=2,'narrow'=8] {'wide_0','wide_1'}, dimensions={0} | all-to-all | bytes 655360 | tf_op jit(solution)/shard_map/all_to_all | solution.py:12
  73.7 0.8 broadcast_in_dim.21
  74.6 3.4 %all-to-all-start.3 = ((bf16[2,32,2,1024]{3,2,1,0:T(2,128)(2,1)}), bf16[2,32,2,1024]{3,2,1,0:T(2,128)(2,1)S(1)}, u32[]{:S(2)}, u32[]{:S(2)}) async-start(bf16[2,32,2,1024]{3,2,1,0:T(2,128)(2,1)} %broadcast_in_dim.21), calls=%async_computation.3 | async-start | bytes 524288 | tf_op jit(solution)/shard_map/all_to_all | solution.py:12
  78.0 0.2 copy.63
  78.2 1.3 all-to-all-done.3
  79.5 0.1 broadcast_in_dim.19
  79.6 4.3 %all_to_all.52 = bf16[2,32,5,1024]{3,1,2,0:T(8,128)(2,1)S(1)} all-to-all(bf16[2,32,5,1024]{3,1,2,0:T(8,128)(2,1)S(1)} %broadcast_in_dim.19), channel_id=1, replica_groups=mesh['wide_0'=2,'wide_1'=16,'wide_2'=2,'narrow'=8] {'wide_2'}, dimensions={0} | all-to-all | bytes 1310720 | tf_op jit(solution)/shard_map/all_to_all | solution.py:12
  83.9 0.9 broadcast_in_dim.22
  84.7 4.4 %all-to-all-start.4 = ((bf16[32,5,1024]{2,1,0:T(8,128)(2,1)}), bf16[32,5,1024]{2,1,0:T(8,128)(2,1)}, u32[]{:S(2)}, u32[]{:S(2)}) async-start(bf16[32,5,1024]{2,1,0:T(8,128)(2,1)} %broadcast_in_dim.22), calls=%async_computation.4 | async-start | bytes 1048576 | tf_op jit(solution)/shard_map/all_to_all | solution.py:12
  89.2 0.2 copy.65
  89.3 0.8 reshape_reshape.13
  90.2 0.4 copy.64
  90.5 0.3 reshape_reshape.12
  90.8 1.4 convolution_dynamic-update-slice_fusion.2
  92.2 1.4 convolution_dynamic-update-slice_fusion.1
  93.6 1.2 convolution_dynamic-update-slice_fusion.4
  94.8 1.1 convolution_dynamic-update-slice_fusion.3
  95.9 27.4 %all-to-all-done.4 = bf16[32,5,1024]{2,1,0:T(8,128)(2,1)} async-done(((bf16[32,5,1024]{2,1,0:T(8,128)(2,1)}), bf16[32,5,1024]{2,1,0:T(8,128)(2,1)}, u32[]{:S(2)}, u32[]{:S(2)}) %all-to-all-start.4) | async-done | bytes 327712 | tf_op jit(solution)/shard_map/all_to_all | solution.py:12
  123.3 1.3 copy.66
  124.6 0.1 broadcast_in_dim.23
  124.7 4.4 %all_to_all.53 = bf16[2,32,5,1024]{3,1,2,0:T(8,128)(2,1)S(1)} all-to-all(bf16[2,32,5,1024]{3,1,2,0:T(8,128)(2,1)S(1)} %broadcast_in_dim.23), channel_id=1, replica_groups=mesh['wide_0'=2,'wide_1'=16,'wide_2'=2,'narrow'=8] {'wide_2'}, dimensions={0} | all-to-all | bytes 1310720 | tf_op jit(solution)/shard_map/all_to_all | solution.py:12
  129.1 0.4 copy.67
  129.4 0.3 reshape_reshape.14
  129.7 1.4 convolution_dynamic-update-slice_fusion
  131.1 3.1 %copy.70 = f32[1216,448]{0,1:T(8,128)} copy(f32[1216,448]{1,0:T(8,128)} %convolution_dynamic-update-slice_fusion) | data formatting | bytes 4358144 | tf_op jit(solution)/shard_map/concatenate | solution.py:39
  134.2 4.5 %all-to-all-start.6 = ((f32[8,1216,56]{1,2,0:T(8,128)}), f32[8,1216,56]{1,2,0:T(8,128)S(1)}, u32[]{:S(2)}, u32[]{:S(2)}) async-start(f32[8,1216,56]{1,2,0:T(8,128)} %bitcast.32), calls=%async_computation.6 | async-start | bytes 4587520 | tf_op jit(solution)/shard_map/all_to_all | solution.py:34
  138.9 0.7 fusion.17
  139.6 33.5 %all-to-all-done.6 = f32[8,1216,56]{1,2,0:T(8,128)S(1)} async-done(((f32[8,1216,56]{1,2,0:T(8,128)}), f32[8,1216,56]{1,2,0:T(8,128)S(1)}, u32[]{:S(2)}, u32[]{:S(2)}) %all-to-all-start.6) | async-done | bytes 2179104 | tf_op jit(solution)/shard_map/all_to_all | solution.py:34
  173.1 0.1 reduce_sum.27
  173.3 0.1 copy.86
  173.4 1.1 gather_fusion.3
  174.5 1.1 gather_fusion.1
  175.6 0.1 copy.85
  175.6 1.1 gather_fusion
  176.7 1.1 gather_fusion.2
  177.8 1.1 gather_fusion.5
  178.9 1.1 gather_fusion.4
  180.0 1.1 gather_fusion.7
  181.1 1.1 gather_fusion.6
  182.2 0.1 copy.76
  182.3 0.1 copy.78
  182.4 0.1 copy.80
  182.5 0.1 copy.74
  182.6 0.1 copy.72
  182.8 0.1 copy.75
  182.9 0.1 copy.77
  183.0 0.1 copy.79
  183.1 5.7 %fusion.14 = bf16[56,320]{1,0:T(8,128)(2,1)S(1)} fusion(f32[1216,56]{0,1:T(8,128)S(1)} %reduce_sum.27, f32[]{:T(128)} %bitcast.5, f32[320,56]{0,1:T(8,128)S(1)} %copy.74, pred[320]{0:T(512)(128)(4,1)S(1)} %get-tuple-element.27, f32[]{:T(128)} %bitcast.6, f32[]{:T(128)} %bitcast.7, f32[]{:T(128)} %bitcast.8, f32[]{:T(128)} %bitcast.9, f32[]{:T(128)} %bitcast.10, ...), kind=kLoop, calls=%fused_computation.102 | loop fusion | flops 4193280 | bytes 467232 | tf_op jit(solution)/shard_map/transpose | solution.py:48
  188.8 6.3 %fusion.15 = bf16[56,320]{1,0:T(8,128)(2,1)S(1)} fusion(f32[320,56]{0,1:T(8,128)S(1)} %copy.79, pred[320]{0:T(512)(128)(4,1)S(1)} %get-tuple-element.24, f32[320,56]{0,1:T(8,128)S(1)} %copy.77, pred[320]{0:T(512)(128)(4,1)S(1)} %get-tuple-element.25, f32[320,56]{0,1:T(8,128)S(1)} %copy.75, pred[320]{0:T(512)(128)(4,1)S(1)} %get-tuple-element.26, ...), kind=kLoop, calls=%fused_computation.103 | loop fusion | flops 7777280 | bytes 825632 | tf_op jit(solution)/shard_map/transpose | solution.py:48
  195.1 0.0 copy-start.2
  195.1 0.1 pad_maximum_fusion
  195.2 12.9 %all_to_all.54 = bf16[8,56,640]{2,1,0:T(8,128)(2,1)S(1)} all-to-all(bf16[8,56,640]{2,1,0:T(8,128)(2,1)S(1)} %stack.2), channel_id=1, replica_groups=mesh['wide_0'=2,'wide_1'=16,'wide_2'=2,'narrow'=8] {'narrow'}, dimensions={0} | all-to-all | bytes 1146880 | tf_op jit(solution)/shard_map/all_to_all | solution.py:53
  208.1 0.5 fusion.1
  208.7 1.7 convolution_add_fusion
  210.4 1.4 reshape_reshape.15
  211.8 0.8 copy.81
  212.6 4.8 %all_to_all.55 = f32[2,32,5,1024]{3,1,2,0:T(8,128)S(1)} all-to-all(f32[2,32,5,1024]{3,1,2,0:T(8,128)S(1)} %copy.81), channel_id=1, replica_groups=mesh['wide_0'=2,'wide_1'=16,'wide_2'=2,'narrow'=8] {'wide_2'}, dimensions={0} | all-to-all | bytes 2621440 | tf_op jit(solution)/shard_map/all_to_all | solution.py:34
  217.4 0.1 reduce_sum.28
  217.5 0.4 copy.82
  217.9 60.9 %all_to_all.56 = f32[32,5,1024]{2,1,0:T(8,128)S(1)} all-to-all(f32[32,5,1024]{2,1,0:T(8,128)S(1)} %copy.82), channel_id=1, replica_groups=mesh['wide_0'=2,'wide_1'=16,'wide_2'=2,'narrow'=8] {'wide_0','wide_1'}, dimensions={0} | all-to-all | bytes 1310720 | tf_op jit(solution)/shard_map/all_to_all | solution.py:67
  278.8 0.7 reduce_sum.29
  (27 shorter events, 0.2 us)
Async XLA Ops:
  0.0 90.8 %copy-start = (bf16[1024,448]{0,1:T(8,128)(2,1)S(1)}, bf16[1024,448]{0,1:T(8,128)(2,1)}, u32[]{:S(2)}) copy-start(bf16[1024,448]{0,1:T(8,128)(2,1)} %param.12) | copy-start | bytes 2752516
  36.8 47.1 %copy-start.5 = (bf16[5,1024]{1,0:T(8,128)(2,1)S(1)}, bf16[5,1024]{1,0:T(8,128)(2,1)}, u32[]{:S(2)}) copy-start(bf16[5,1024]{1,0:T(8,128)(2,1)} %param.15) | copy-start | bytes 30724
  74.6 5.0 %all-to-all-start.3 = ((bf16[2,32,2,1024]{3,2,1,0:T(2,128)(2,1)}), bf16[2,32,2,1024]{3,2,1,0:T(2,128)(2,1)S(1)}, u32[]{:S(2)}, u32[]{:S(2)}) async-start(bf16[2,32,2,1024]{3,2,1,0:T(2,128)(2,1)} %broadcast_in_dim.21), calls=%async_computation.3 | async-start | bytes 524288 | tf_op jit(solution)/shard_map/all_to_all | solution.py:12
  84.7 38.6 %all-to-all-start.4 = ((bf16[32,5,1024]{2,1,0:T(8,128)(2,1)}), bf16[32,5,1024]{2,1,0:T(8,128)(2,1)}, u32[]{:S(2)}, u32[]{:S(2)}) async-start(bf16[32,5,1024]{2,1,0:T(8,128)(2,1)} %broadcast_in_dim.22), calls=%async_computation.4 | async-start | bytes 1048576 | tf_op jit(solution)/shard_map/all_to_all | solution.py:12
  90.2 2.1 copy-start.1
  90.8 2.8 copy-start.3
  124.6 5.1 %copy-start.4 = (bf16[448,1024]{1,0:T(8,128)(2,1)S(1)}, bf16[448,1024]{1,0:T(8,128)(2,1)}, u32[]{:S(2)}) copy-start(bf16[448,1024]{1,0:T(8,128)(2,1)} %param.14) | copy-start | bytes 2752516
  134.2 4.6 %copy-start.6 = (s32[320,4]{0,1:T(4,128)S(1)}, s32[320,4]{0,1:T(4,128)}, u32[]{:S(2)}) copy-start(s32[320,4]{0,1:T(4,128)} %param.16) | copy-start | bytes 15364
  134.2 4.7 %copy-start.7 = (s32[8]{0:T(128)S(1)}, s32[8]{0:T(128)}, u32[]{:S(2)}) copy-start(s32[8]{0:T(128)} %param.17) | copy-start | bytes 100
  134.2 38.9 %all-to-all-start.6 = ((f32[8,1216,56]{1,2,0:T(8,128)}), f32[8,1216,56]{1,2,0:T(8,128)S(1)}, u32[]{:S(2)}, u32[]{:S(2)}) async-start(f32[8,1216,56]{1,2,0:T(8,128)} %bitcast.32), calls=%async_computation.6 | async-start | bytes 4587520 | tf_op jit(solution)/shard_map/all_to_all | solution.py:34
  195.1 13.6 %copy-start.2 = (bf16[1024,448]{0,1:T(8,128)(2,1)S(1)}, bf16[1024,448]{0,1:T(8,128)(2,1)}, u32[]{:S(2)}) copy-start(bf16[1024,448]{0,1:T(8,128)(2,1)} %param.13) | copy-start | bytes 2752516
